TPU v7x, 32 devices: a whole 2x2x4 slice. The times are simulated.
32 devices in a mesh: tm: 4 (over y, core), space: 8 (over z, x).
Axes of the slice: x: 2, y: 2, z: 4, core: 2. Of those that a mesh axis runs over, the one named last changes fastest.
Arguments:
- node_states: float32 [4, 9, 32768], P('tm', None, 'space'), may hold values from -6 to 6
- strengths: float32 [3, 32768], P(None, 'space'), may hold values from -4 to 4
- start_state: float32 [3, 32768], P(None, 'space'), may hold values from -6 to 6
- lists: int32 [256, 12], replicated, may hold values from 0 to 255, as said below
- counts: int32 [8], replicated, may hold values from 16 to 32, as said below
Outputs:
- new_nodes: float32 [4, 9, 32768], P('tm', None, 'space')
Inputs may be any that keep to these rules, and one draw needn't show every extreme that they name: `lists`: every entry names a live block; the entries of one row are distinct; over all rows of one shard, live or not, each other shard has between 1 and 2 distinct blocks named, and some pair of shards reaches 2; a shard's own blocks may be named freely. `counts`: number of live blocks of each shard; slots from that number to 31 hold no particles that matter.
All inputs are finite; a program needn't handle non-finite values.
Results may differ from a plain program's by a relative error of at most 0.00005.
Values sent between devices are 32-bit elements; how exact they have to be, the bound alone decides.
A program may use at most 64 MiB of HBM per device.

v0:
```python
import math

import jax
import jax.numpy as jnp
import numpy as np
from jax import lax
from jax.sharding import PartitionSpec as P

core_sq = 0.25
step_size = 1.0
group_size = 2


def entering(value, axis, join, neutral):
    count, mine = (lax.axis_size(axis), lax.axis_index(axis))
    pieces = lax.all_gather(value, axis)
    subtotal = jnp.full_like(value, 0) + jnp.asarray(neutral, value.dtype)

    def step(position, subtotal):
        longer = join(subtotal, pieces[position])
        return jnp.where(position < mine, longer, subtotal)

    return lax.fori_loop(0, count - 1, step, subtotal)


def radau_matrix():
    sqrt_six = math.sqrt(6.0)
    return np.array(
        [
            [
                (88.0 - 7.0 * sqrt_six) / 360.0,
                (296.0 - 169.0 * sqrt_six) / 1800.0,
                (-2.0 + 3.0 * sqrt_six) / 225.0,
            ],
            [
                (296.0 + 169.0 * sqrt_six) / 1800.0,
                (88.0 + 7.0 * sqrt_six) / 360.0,
                (-2.0 - 3.0 * sqrt_six) / 225.0,
            ],
            [(16.0 - sqrt_six) / 36.0, (16.0 + sqrt_six) / 36.0, 1.0 / 9.0],
        ]
    )


def cross_rows(former, latter):
    return jnp.stack(
        [
            former[:, 1] * latter[:, 2] - former[:, 2] * latter[:, 1],
            former[:, 2] * latter[:, 0] - former[:, 0] * latter[:, 2],
            former[:, 0] * latter[:, 1] - former[:, 1] * latter[:, 0],
        ],
        axis=1,
    )


def block_velocity(targets, sources):
    listed = jnp.transpose(sources, (1, 0, 2)).reshape(12, -1)
    places = listed[:9].reshape(3, 3, -1)
    strength = jnp.broadcast_to(listed[9:][None], places.shape)
    target_pos = targets.reshape(3, 3, -1)
    offset = target_pos[:, :, None, :] - places[:, :, :, None]
    kernel = (jnp.sum(offset * offset, axis=1) + core_sq) ** (-1.5)
    weights = jnp.concatenate([strength, cross_rows(places, strength)], axis=1)
    totals = jnp.einsum("mks,msb->mkb", weights, kernel, precision=lax.Precision.HIGHEST)
    spread = cross_rows(target_pos, totals[:, :3]) - totals[:, 3:]
    return (spread * (-0.25 / math.pi)).reshape(9, -1)


def shards(node_states, strengths, start_state, lists, counts):
    groups = lax.axis_size("space")
    rank_space = lax.axis_index("space")
    blocks_dev = lists.shape[0] // groups
    block_size = node_states.shape[2] // blocks_dev
    list_len = lists.shape[1]
    payload = jnp.concatenate([node_states[0], strengths], axis=0)
    own_blocks = payload.reshape(12, blocks_dev, block_size).transpose(1, 0, 2)
    my_lists = lax.dynamic_slice_in_dim(lists, rank_space * blocks_dev, blocks_dev, 0)
    source_table = lax.all_gather(own_blocks, "space", axis=0, tiled=True)
    targets_all = node_states[0].reshape(9, blocks_dev, block_size).transpose(1, 0, 2)
    live_count = lax.dynamic_index_in_dim(counts, rank_space, 0, keepdims=False)

    def one_group(packed):
        group_slots, group_targets = packed
        group_sources = jnp.take(source_table, group_slots.reshape(-1), axis=0)
        group_sources = group_sources.reshape(
            group_slots.shape[0], group_slots.shape[1], 12, block_size
        )
        return jax.vmap(block_velocity)(group_targets, group_sources)

    steps_count = blocks_dev // group_size
    velocity = lax.map(
        one_group,
        (
            my_lists.reshape(steps_count, group_size, list_len),
            targets_all.reshape(steps_count, group_size, 9, block_size),
        ),
    )
    velocity = velocity.reshape(blocks_dev, 9, block_size)
    live_rows = jnp.arange(blocks_dev, dtype=jnp.int32) < live_count
    velocity = jnp.where(live_rows[:, None, None], velocity, jnp.zeros_like(velocity))
    rates = velocity.transpose(1, 0, 2).reshape(3, 3, blocks_dev * block_size)
    table = jnp.asarray(radau_matrix(), jnp.float32)
    quadrature = step_size * jnp.einsum(
        "mj,jcp->mcp", table, rates, precision=lax.Precision.HIGHEST
    )
    increment = quadrature[2]
    carried = entering(
        increment, "tm", lambda earlier, coming: earlier + coming, jnp.zeros_like(increment)
    )
    updated = start_state + carried + quadrature
    return updated.reshape(1, 9, -1)


def solution(mesh):
    return jax.shard_map(
        shards,
        mesh=mesh,
        in_specs=(P("tm", None, "space"), P(None, "space"), P(None, "space"), P(), P()),
        out_specs=P("tm", None, "space"),
        check_vma=False,
    )
```

profile of v0, /device:TPU:0, one launch (start us, length us, event | category | flops | bytes accessed | tf_op | source)
XLA Modules:
  0.0 248.3 jit_solution(4642739917644568281)
XLA Ops:
  6.5 0.9 copy.97
  7.4 1.6 maximum_bitcast_fusion
  9.2 1.3 dynamic_slice.22
  11.1 45.3 %all-gather.2.cloned.1.call-done = f32[256,12,128]{2,0,1:T(8,128)} async-done(((f32[32,12,128]{2,0,1:T(8,128)}), f32[256,12,128]{2,0,1:T(8,128)}) %all-gather.2.cloned.1.call-update) | async-done | bytes 1572880 | tf_op jit(solution)/shard_map/all_gather | solution.py:78
  56.5 2.4 copy.81
  58.8 174.8 %while.24 = (s32[]{:T(128)}, f32[16,2,9,128]{3,1,0,2:T(2,128)S(1)}, f32[16,2,9,128]{3,1,0,2:T(2,128)}, s32[16,2,12]{2,1,0:T(2,128)S(1)}, f32[256,12,128]{2,1,0:T(8,128)S(1)}, /*index=5*/s32[]{:T(128)}) while((s32[]{:T(128)}, f32[16,2,9,128]{3,1,0,2:T(2,128)S(1)}, f32[16,2,9,128]{3,1,0,2:T(2,128)}, s32[16,2,12]{2,1,0:T(2,128)S(1)}, ...), condition=%wide.region_2.3_spmd, body=%wide.region_0.2_spmd.sunk | while | flops 95854552 | bytes 11884417 | solution.py:91
  59.9 0.7 constant_dynamic-slice_fusion.5
  60.7 4.7 %multiply_reduce_fusion.2 = f32[2,3,1536,128]{3,2,1,0:T(8,128)S(1)} fusion(f32[2,3,3,1536]{3,2,1,0:T(4,128)S(1)} %copy.104, f32[2,3,3,128]{3,2,1,0:T(4,128)S(1)} %copy.105), kind=kLoop, calls=%fused_computation.1.clone.1 | loop fusion | flops 9437184 | bytes 4838400 | tf_op jit(solution)/shard_map/while/body/eval_jaxpr/vmap()/reduce_sum | solution.py:62
  65.4 4.2 %fusion.31 = f32[2,3,6,128]{3,2,1,0:T(8,128)S(1)} fusion(f32[2,3,1536,128]{3,2,1,0:T(8,128)S(1)} %multiply_reduce_fusion.2, f32[2,3,1,1536]{3,2,1,0:T(1,128)S(1)} %get-tuple-element.257, f32[2,3,1,1536]{3,2,1,0:T(1,128)S(1)} %get-tuple-element.258, f32[2,3,1,1536]{3,2,1,0:T(1,128)S(1)} %get-tuple-element.259, f32[2,3,3,1536]{3,2,1,0:T(4,128)S(1)} %broadcast_in_dim.68), kind=kOutput, calls=%fused_computation.2.clone.1 | convolution fusion | flops 86280192 | bytes 4958208 | tf_op jit(solution)/shard_map/while/body/eval_jaxpr/vmap(mks,msb->mkb)/dot_general | solution.py:64
  70.9 0.7 constant_dynamic-slice_fusion.5
  71.6 4.7 %multiply_reduce_fusion.2 = f32[2,3,1536,128]{3,2,1,0:T(8,128)S(1)} fusion(f32[2,3,3,1536]{3,2,1,0:T(4,128)S(1)} %copy.104, f32[2,3,3,128]{3,2,1,0:T(4,128)S(1)} %copy.105), kind=kLoop, calls=%fused_computation.1.clone.1 | loop fusion | flops 9437184 | bytes 4838400 | tf_op jit(solution)/shard_map/while/body/eval_jaxpr/vmap()/reduce_sum | solution.py:62
  76.4 4.2 %fusion.31 = f32[2,3,6,128]{3,2,1,0:T(8,128)S(1)} fusion(f32[2,3,1536,128]{3,2,1,0:T(8,128)S(1)} %multiply_reduce_fusion.2, f32[2,3,1,1536]{3,2,1,0:T(1,128)S(1)} %get-tuple-element.257, f32[2,3,1,1536]{3,2,1,0:T(1,128)S(1)} %get-tuple-element.258, f32[2,3,1,1536]{3,2,1,0:T(1,128)S(1)} %get-tuple-element.259, f32[2,3,3,1536]{3,2,1,0:T(4,128)S(1)} %broadcast_in_dim.68), kind=kOutput, calls=%fused_computation.2.clone.1 | convolution fusion | flops 86280192 | bytes 4958208 | tf_op jit(solution)/shard_map/while/body/eval_jaxpr/vmap(mks,msb->mkb)/dot_general | solution.py:64
  81.8 0.7 constant_dynamic-slice_fusion.5
  82.5 4.7 %multiply_reduce_fusion.2 = f32[2,3,1536,128]{3,2,1,0:T(8,128)S(1)} fusion(f32[2,3,3,1536]{3,2,1,0:T(4,128)S(1)} %copy.104, f32[2,3,3,128]{3,2,1,0:T(4,128)S(1)} %copy.105), kind=kLoop, calls=%fused_computation.1.clone.1 | loop fusion | flops 9437184 | bytes 4838400 | tf_op jit(solution)/shard_map/while/body/eval_jaxpr/vmap()/reduce_sum | solution.py:62
  87.3 4.2 %fusion.31 = f32[2,3,6,128]{3,2,1,0:T(8,128)S(1)} fusion(f32[2,3,1536,128]{3,2,1,0:T(8,128)S(1)} %multiply_reduce_fusion.2, f32[2,3,1,1536]{3,2,1,0:T(1,128)S(1)} %get-tuple-element.257, f32[2,3,1,1536]{3,2,1,0:T(1,128)S(1)} %get-tuple-element.258, f32[2,3,1,1536]{3,2,1,0:T(1,128)S(1)} %get-tuple-element.259, f32[2,3,3,1536]{3,2,1,0:T(4,128)S(1)} %broadcast_in_dim.68), kind=kOutput, calls=%fused_computation.2.clone.1 | convolution fusion | flops 86280192 | bytes 4958208 | tf_op jit(solution)/shard_map/while/body/eval_jaxpr/vmap(mks,msb->mkb)/dot_general | solution.py:64
  92.7 0.7 constant_dynamic-slice_fusion.5
  93.5 4.7 %multiply_reduce_fusion.2 = f32[2,3,1536,128]{3,2,1,0:T(8,128)S(1)} fusion(f32[2,3,3,1536]{3,2,1,0:T(4,128)S(1)} %copy.104, f32[2,3,3,128]{3,2,1,0:T(4,128)S(1)} %copy.105), kind=kLoop, calls=%fused_computation.1.clone.1 | loop fusion | flops 9437184 | bytes 4838400 | tf_op jit(solution)/shard_map/while/body/eval_jaxpr/vmap()/reduce_sum | solution.py:62
  98.3 4.2 %fusion.31 = f32[2,3,6,128]{3,2,1,0:T(8,128)S(1)} fusion(f32[2,3,1536,128]{3,2,1,0:T(8,128)S(1)} %multiply_reduce_fusion.2, f32[2,3,1,1536]{3,2,1,0:T(1,128)S(1)} %get-tuple-element.257, f32[2,3,1,1536]{3,2,1,0:T(1,128)S(1)} %get-tuple-element.258, f32[2,3,1,1536]{3,2,1,0:T(1,128)S(1)} %get-tuple-element.259, f32[2,3,3,1536]{3,2,1,0:T(4,128)S(1)} %broadcast_in_dim.68), kind=kOutput, calls=%fused_computation.2.clone.1 | convolution fusion | flops 86280192 | bytes 4958208 | tf_op jit(solution)/shard_map/while/body/eval_jaxpr/vmap(mks,msb->mkb)/dot_general | solution.py:64
  103.7 0.7 constant_dynamic-slice_fusion.5
  104.4 4.7 %multiply_reduce_fusion.2 = f32[2,3,1536,128]{3,2,1,0:T(8,128)S(1)} fusion(f32[2,3,3,1536]{3,2,1,0:T(4,128)S(1)} %copy.104, f32[2,3,3,128]{3,2,1,0:T(4,128)S(1)} %copy.105), kind=kLoop, calls=%fused_computation.1.clone.1 | loop fusion | flops 9437184 | bytes 4838400 | tf_op jit(solution)/shard_map/while/body/eval_jaxpr/vmap()/reduce_sum | solution.py:62
  109.2 4.2 %fusion.31 = f32[2,3,6,128]{3,2,1,0:T(8,128)S(1)} fusion(f32[2,3,1536,128]{3,2,1,0:T(8,128)S(1)} %multiply_reduce_fusion.2, f32[2,3,1,1536]{3,2,1,0:T(1,128)S(1)} %get-tuple-element.257, f32[2,3,1,1536]{3,2,1,0:T(1,128)S(1)} %get-tuple-element.258, f32[2,3,1,1536]{3,2,1,0:T(1,128)S(1)} %get-tuple-element.259, f32[2,3,3,1536]{3,2,1,0:T(4,128)S(1)} %broadcast_in_dim.68), kind=kOutput, calls=%fused_computation.2.clone.1 | convolution fusion | flops 86280192 | bytes 4958208 | tf_op jit(solution)/shard_map/while/body/eval_jaxpr/vmap(mks,msb->mkb)/dot_general | solution.py:64
  115.3 4.7 %multiply_reduce_fusion.2 = f32[2,3,1536,128]{3,2,1,0:T(8,128)S(1)} fusion(f32[2,3,3,1536]{3,2,1,0:T(4,128)S(1)} %copy.104, f32[2,3,3,128]{3,2,1,0:T(4,128)S(1)} %copy.105), kind=kLoop, calls=%fused_computation.1.clone.1 | loop fusion | flops 9437184 | bytes 4838400 | tf_op jit(solution)/shard_map/while/body/eval_jaxpr/vmap()/reduce_sum | solution.py:62
  120.1 4.2 %fusion.31 = f32[2,3,6,128]{3,2,1,0:T(8,128)S(1)} fusion(f32[2,3,1536,128]{3,2,1,0:T(8,128)S(1)} %multiply_reduce_fusion.2, f32[2,3,1,1536]{3,2,1,0:T(1,128)S(1)} %get-tuple-element.257, f32[2,3,1,1536]{3,2,1,0:T(1,128)S(1)} %get-tuple-element.258, f32[2,3,1,1536]{3,2,1,0:T(1,128)S(1)} %get-tuple-element.259, f32[2,3,3,1536]{3,2,1,0:T(4,128)S(1)} %broadcast_in_dim.68), kind=kOutput, calls=%fused_computation.2.clone.1 | convolution fusion | flops 86280192 | bytes 4958208 | tf_op jit(solution)/shard_map/while/body/eval_jaxpr/vmap(mks,msb->mkb)/dot_general | solution.py:64
  125.5 0.7 constant_dynamic-slice_fusion.5
  126.2 4.7 %multiply_reduce_fusion.2 = f32[2,3,1536,128]{3,2,1,0:T(8,128)S(1)} fusion(f32[2,3,3,1536]{3,2,1,0:T(4,128)S(1)} %copy.104, f32[2,3,3,128]{3,2,1,0:T(4,128)S(1)} %copy.105), kind=kLoop, calls=%fused_computation.1.clone.1 | loop fusion | flops 9437184 | bytes 4838400 | tf_op jit(solution)/shard_map/while/body/eval_jaxpr/vmap()/reduce_sum | solution.py:62
  131.0 4.2 %fusion.31 = f32[2,3,6,128]{3,2,1,0:T(8,128)S(1)} fusion(f32[2,3,1536,128]{3,2,1,0:T(8,128)S(1)} %multiply_reduce_fusion.2, f32[2,3,1,1536]{3,2,1,0:T(1,128)S(1)} %get-tuple-element.257, f32[2,3,1,1536]{3,2,1,0:T(1,128)S(1)} %get-tuple-element.258, f32[2,3,1,1536]{3,2,1,0:T(1,128)S(1)} %get-tuple-element.259, f32[2,3,3,1536]{3,2,1,0:T(4,128)S(1)} %broadcast_in_dim.68), kind=kOutput, calls=%fused_computation.2.clone.1 | convolution fusion | flops 86280192 | bytes 4958208 | tf_op jit(solution)/shard_map/while/body/eval_jaxpr/vmap(mks,msb->mkb)/dot_general | solution.py:64
  137.1 4.7 %multiply_reduce_fusion.2 = f32[2,3,1536,128]{3,2,1,0:T(8,128)S(1)} fusion(f32[2,3,3,1536]{3,2,1,0:T(4,128)S(1)} %copy.104, f32[2,3,3,128]{3,2,1,0:T(4,128)S(1)} %copy.105), kind=kLoop, calls=%fused_computation.1.clone.1 | loop fusion | flops 9437184 | bytes 4838400 | tf_op jit(solution)/shard_map/while/body/eval_jaxpr/vmap()/reduce_sum | solution.py:62
  141.9 4.2 %fusion.31 = f32[2,3,6,128]{3,2,1,0:T(8,128)S(1)} fusion(f32[2,3,1536,128]{3,2,1,0:T(8,128)S(1)} %multiply_reduce_fusion.2, f32[2,3,1,1536]{3,2,1,0:T(1,128)S(1)} %get-tuple-element.257, f32[2,3,1,1536]{3,2,1,0:T(1,128)S(1)} %get-tuple-element.258, f32[2,3,1,1536]{3,2,1,0:T(1,128)S(1)} %get-tuple-element.259, f32[2,3,3,1536]{3,2,1,0:T(4,128)S(1)} %broadcast_in_dim.68), kind=kOutput, calls=%fused_computation.2.clone.1 | convolution fusion | flops 86280192 | bytes 4958208 | tf_op jit(solution)/shard_map/while/body/eval_jaxpr/vmap(mks,msb->mkb)/dot_general | solution.py:64
  148.1 4.7 %multiply_reduce_fusion.2 = f32[2,3,1536,128]{3,2,1,0:T(8,128)S(1)} fusion(f32[2,3,3,1536]{3,2,1,0:T(4,128)S(1)} %copy.104, f32[2,3,3,128]{3,2,1,0:T(4,128)S(1)} %copy.105), kind=kLoop, calls=%fused_computation.1.clone.1 | loop fusion | flops 9437184 | bytes 4838400 | tf_op jit(solution)/shard_map/while/body/eval_jaxpr/vmap()/reduce_sum | solution.py:62
  152.8 4.2 %fusion.31 = f32[2,3,6,128]{3,2,1,0:T(8,128)S(1)} fusion(f32[2,3,1536,128]{3,2,1,0:T(8,128)S(1)} %multiply_reduce_fusion.2, f32[2,3,1,1536]{3,2,1,0:T(1,128)S(1)} %get-tuple-element.257, f32[2,3,1,1536]{3,2,1,0:T(1,128)S(1)} %get-tuple-element.258, f32[2,3,1,1536]{3,2,1,0:T(1,128)S(1)} %get-tuple-element.259, f32[2,3,3,1536]{3,2,1,0:T(4,128)S(1)} %broadcast_in_dim.68), kind=kOutput, calls=%fused_computation.2.clone.1 | convolution fusion | flops 86280192 | bytes 4958208 | tf_op jit(solution)/shard_map/while/body/eval_jaxpr/vmap(mks,msb->mkb)/dot_general | solution.py:64
  158.3 0.7 constant_dynamic-slice_fusion.5
  159.0 4.7 %multiply_reduce_fusion.2 = f32[2,3,1536,128]{3,2,1,0:T(8,128)S(1)} fusion(f32[2,3,3,1536]{3,2,1,0:T(4,128)S(1)} %copy.104, f32[2,3,3,128]{3,2,1,0:T(4,128)S(1)} %copy.105), kind=kLoop, calls=%fused_computation.1.clone.1 | loop fusion | flops 9437184 | bytes 4838400 | tf_op jit(solution)/shard_map/while/body/eval_jaxpr/vmap()/reduce_sum | solution.py:62
  163.8 4.2 %fusion.31 = f32[2,3,6,128]{3,2,1,0:T(8,128)S(1)} fusion(f32[2,3,1536,128]{3,2,1,0:T(8,128)S(1)} %multiply_reduce_fusion.2, f32[2,3,1,1536]{3,2,1,0:T(1,128)S(1)} %get-tuple-element.257, f32[2,3,1,1536]{3,2,1,0:T(1,128)S(1)} %get-tuple-element.258, f32[2,3,1,1536]{3,2,1,0:T(1,128)S(1)} %get-tuple-element.259, f32[2,3,3,1536]{3,2,1,0:T(4,128)S(1)} %broadcast_in_dim.68), kind=kOutput, calls=%fused_computation.2.clone.1 | convolution fusion | flops 86280192 | bytes 4958208 | tf_op jit(solution)/shard_map/while/body/eval_jaxpr/vmap(mks,msb->mkb)/dot_general | solution.py:64
  169.2 0.7 constant_dynamic-slice_fusion.5
  169.9 4.7 %multiply_reduce_fusion.2 = f32[2,3,1536,128]{3,2,1,0:T(8,128)S(1)} fusion(f32[2,3,3,1536]{3,2,1,0:T(4,128)S(1)} %copy.104, f32[2,3,3,128]{3,2,1,0:T(4,128)S(1)} %copy.105), kind=kLoop, calls=%fused_computation.1.clone.1 | loop fusion | flops 9437184 | bytes 4838400 | tf_op jit(solution)/shard_map/while/body/eval_jaxpr/vmap()/reduce_sum | solution.py:62
  174.7 4.2 %fusion.31 = f32[2,3,6,128]{3,2,1,0:T(8,128)S(1)} fusion(f32[2,3,1536,128]{3,2,1,0:T(8,128)S(1)} %multiply_reduce_fusion.2, f32[2,3,1,1536]{3,2,1,0:T(1,128)S(1)} %get-tuple-element.257, f32[2,3,1,1536]{3,2,1,0:T(1,128)S(1)} %get-tuple-element.258, f32[2,3,1,1536]{3,2,1,0:T(1,128)S(1)} %get-tuple-element.259, f32[2,3,3,1536]{3,2,1,0:T(4,128)S(1)} %broadcast_in_dim.68), kind=kOutput, calls=%fused_computation.2.clone.1 | convolution fusion | flops 86280192 | bytes 4958208 | tf_op jit(solution)/shard_map/while/body/eval_jaxpr/vmap(mks,msb->mkb)/dot_general | solution.py:64
  180.8 4.7 %multiply_reduce_fusion.2 = f32[2,3,1536,128]{3,2,1,0:T(8,128)S(1)} fusion(f32[2,3,3,1536]{3,2,1,0:T(4,128)S(1)} %copy.104, f32[2,3,3,128]{3,2,1,0:T(4,128)S(1)} %copy.105), kind=kLoop, calls=%fused_computation.1.clone.1 | loop fusion | flops 9437184 | bytes 4838400 | tf_op jit(solution)/shard_map/while/body/eval_jaxpr/vmap()/reduce_sum | solution.py:62
  185.6 4.2 %fusion.31 = f32[2,3,6,128]{3,2,1,0:T(8,128)S(1)} fusion(f32[2,3,1536,128]{3,2,1,0:T(8,128)S(1)} %multiply_reduce_fusion.2, f32[2,3,1,1536]{3,2,1,0:T(1,128)S(1)} %get-tuple-element.257, f32[2,3,1,1536]{3,2,1,0:T(1,128)S(1)} %get-tuple-element.258, f32[2,3,1,1536]{3,2,1,0:T(1,128)S(1)} %get-tuple-element.259, f32[2,3,3,1536]{3,2,1,0:T(4,128)S(1)} %broadcast_in_dim.68), kind=kOutput, calls=%fused_computation.2.clone.1 | convolution fusion | flops 86280192 | bytes 4958208 | tf_op jit(solution)/shard_map/while/body/eval_jaxpr/vmap(mks,msb->mkb)/dot_general | solution.py:64
  191.8 4.7 %multiply_reduce_fusion.2 = f32[2,3,1536,128]{3,2,1,0:T(8,128)S(1)} fusion(f32[2,3,3,1536]{3,2,1,0:T(4,128)S(1)} %copy.104, f32[2,3,3,128]{3,2,1,0:T(4,128)S(1)} %copy.105), kind=kLoop, calls=%fused_computation.1.clone.1 | loop fusion | flops 9437184 | bytes 4838400 | tf_op jit(solution)/shard_map/while/body/eval_jaxpr/vmap()/reduce_sum | solution.py:62
  196.5 4.2 %fusion.31 = f32[2,3,6,128]{3,2,1,0:T(8,128)S(1)} fusion(f32[2,3,1536,128]{3,2,1,0:T(8,128)S(1)} %multiply_reduce_fusion.2, f32[2,3,1,1536]{3,2,1,0:T(1,128)S(1)} %get-tuple-element.257, f32[2,3,1,1536]{3,2,1,0:T(1,128)S(1)} %get-tuple-element.258, f32[2,3,1,1536]{3,2,1,0:T(1,128)S(1)} %get-tuple-element.259, f32[2,3,3,1536]{3,2,1,0:T(4,128)S(1)} %broadcast_in_dim.68), kind=kOutput, calls=%fused_computation.2.clone.1 | convolution fusion | flops 86280192 | bytes 4958208 | tf_op jit(solution)/shard_map/while/body/eval_jaxpr/vmap(mks,msb->mkb)/dot_general | solution.py:64
  202.7 4.7 %multiply_reduce_fusion.2 = f32[2,3,1536,128]{3,2,1,0:T(8,128)S(1)} fusion(f32[2,3,3,1536]{3,2,1,0:T(4,128)S(1)} %copy.104, f32[2,3,3,128]{3,2,1,0:T(4,128)S(1)} %copy.105), kind=kLoop, calls=%fused_computation.1.clone.1 | loop fusion | flops 9437184 | bytes 4838400 | tf_op jit(solution)/shard_map/while/body/eval_jaxpr/vmap()/reduce_sum | solution.py:62
  207.5 4.2 %fusion.31 = f32[2,3,6,128]{3,2,1,0:T(8,128)S(1)} fusion(f32[2,3,1536,128]{3,2,1,0:T(8,128)S(1)} %multiply_reduce_fusion.2, f32[2,3,1,1536]{3,2,1,0:T(1,128)S(1)} %get-tuple-element.257, f32[2,3,1,1536]{3,2,1,0:T(1,128)S(1)} %get-tuple-element.258, f32[2,3,1,1536]{3,2,1,0:T(1,128)S(1)} %get-tuple-element.259, f32[2,3,3,1536]{3,2,1,0:T(4,128)S(1)} %broadcast_in_dim.68), kind=kOutput, calls=%fused_computation.2.clone.1 | convolution fusion | flops 86280192 | bytes 4958208 | tf_op jit(solution)/shard_map/while/body/eval_jaxpr/vmap(mks,msb->mkb)/dot_general | solution.py:64
  213.6 4.7 %multiply_reduce_fusion.2 = f32[2,3,1536,128]{3,2,1,0:T(8,128)S(1)} fusion(f32[2,3,3,1536]{3,2,1,0:T(4,128)S(1)} %copy.104, f32[2,3,3,128]{3,2,1,0:T(4,128)S(1)} %copy.105), kind=kLoop, calls=%fused_computation.1.clone.1 | loop fusion | flops 9437184 | bytes 4838400 | tf_op jit(solution)/shard_map/while/body/eval_jaxpr/vmap()/reduce_sum | solution.py:62
  218.4 4.2 %fusion.31 = f32[2,3,6,128]{3,2,1,0:T(8,128)S(1)} fusion(f32[2,3,1536,128]{3,2,1,0:T(8,128)S(1)} %multiply_reduce_fusion.2, f32[2,3,1,1536]{3,2,1,0:T(1,128)S(1)} %get-tuple-element.257, f32[2,3,1,1536]{3,2,1,0:T(1,128)S(1)} %get-tuple-element.258, f32[2,3,1,1536]{3,2,1,0:T(1,128)S(1)} %get-tuple-element.259, f32[2,3,3,1536]{3,2,1,0:T(4,128)S(1)} %broadcast_in_dim.68), kind=kOutput, calls=%fused_computation.2.clone.1 | convolution fusion | flops 86280192 | bytes 4958208 | tf_op jit(solution)/shard_map/while/body/eval_jaxpr/vmap(mks,msb->mkb)/dot_general | solution.py:64
  224.5 4.7 %multiply_reduce_fusion.2 = f32[2,3,1536,128]{3,2,1,0:T(8,128)S(1)} fusion(f32[2,3,3,1536]{3,2,1,0:T(4,128)S(1)} %copy.104, f32[2,3,3,128]{3,2,1,0:T(4,128)S(1)} %copy.105), kind=kLoop, calls=%fused_computation.1.clone.1 | loop fusion | flops 9437184 | bytes 4838400 | tf_op jit(solution)/shard_map/while/body/eval_jaxpr/vmap()/reduce_sum | solution.py:62
  229.3 4.2 %fusion.31 = f32[2,3,6,128]{3,2,1,0:T(8,128)S(1)} fusion(f32[2,3,1536,128]{3,2,1,0:T(8,128)S(1)} %multiply_reduce_fusion.2, f32[2,3,1,1536]{3,2,1,0:T(1,128)S(1)} %get-tuple-element.257, f32[2,3,1,1536]{3,2,1,0:T(1,128)S(1)} %get-tuple-element.258, f32[2,3,1,1536]{3,2,1,0:T(1,128)S(1)} %get-tuple-element.259, f32[2,3,3,1536]{3,2,1,0:T(4,128)S(1)} %broadcast_in_dim.68), kind=kOutput, calls=%fused_computation.2.clone.1 | convolution fusion | flops 86280192 | bytes 4958208 | tf_op jit(solution)/shard_map/while/body/eval_jaxpr/vmap(mks,msb->mkb)/dot_general | solution.py:64
  234.4 5.8 %all_gather.7 = f32[4,3,4096]{2,1,0:T(4,128)S(1)} all-gather(f32[1,3,4096]{2,1,0:T(4,128)S(1)} %copy.84), channel_id=1, replica_groups=mesh['tm'=4,'space'=8] {'tm'}, dimensions={0}, use_global_device_ids=true | all-gather | bytes 245760 | tf_op jit(solution)/shard_map/all_gather | solution.py:16
  240.6 0.9 reshape.103
  (337 shorter events, 26.4 us)
Async XLA Ops:
  6.5 2.5 %copy-start = (s32[256,12]{0,1:T(8,128)S(1)}, s32[256,12]{0,1:T(8,128)}, u32[]{:S(2)}) copy-start(s32[256,12]{0,1:T(8,128)} %param.13) | copy-start | bytes 36868
  6.5 49.9 %all-gather.2.cloned.1.call-start = ((), (), s32[]{:S(2)}) async-start(), calls=%async_computation | async-start | bytes 1769472 | tf_op jit(solution)/shard_map/all_gather | solution.py:78
  58.8 175.0 %copy-start.2 = (f32[3,3,1]{1,0,2:T(4,128)S(1)}, f32[3,3,1]{1,0,2:T(4,128)}, u32[]{:S(2)}) copy-start(f32[3,3,1]{1,0,2:T(4,128)} %constant.83) | copy-start | bytes 112
  58.8 181.6 %copy-start.1 = (f32[3,4096]{1,0:T(4,128)S(1)}, f32[3,4096]{1,0:T(4,128)}, u32[]{:S(2)}) copy-start(f32[3,4096]{1,0:T(4,128)} %param.12) | copy-start | bytes 147460
Sparse Core Ops, SparseCore 0:
  9.5 46.8 all-gather.1
where the time goes:
time: 249 us; the launch traced here: 248 us
  other arithmetic  82.9 us (33%)
  matrix products  67.8 us (27%)
  waiting for transfers between devices  45.3 us (18%)
  local copies, waits for them, and re-layouts  30.9 us (12%)
  between operations  13.5 us (5%)
  blocking collectives  5.79 us (2%)
    reduce_sum x16, other arithmetic, block_velocity(): kernel = (jnp.sum(offset * offset, axis=1) + core_sq) ** (-1.5)  75.5 us
    dot_general x16, matrix products, block_velocity(): jnp.einsum('mks,msb->mkb', weights, kernel, precision=lax.Precision.HIGHEST)  67.3 us
    all_gather x1, waiting for transfers between devices, shards(): source_table = lax.all_gather(own_blocks, 'space', axis=0, tiled=True)  45.3 us
    dynamic_slice x16, local copies, waits for them, and re-layouts, shards(): lax.map(one_group, (my_lists.reshape(steps_count, group_size, list_len),...  11.4 us
    gather x16, local copies, waits for them, and re-layouts, one_group(): group_sources = jnp.take(source_table, group_slots.reshape(-1), axis=0)  9.21 us
    all_gather x1, blocking collectives, entering(): pieces = lax.all_gather(value, axis)  5.79 us
  transfers between devices with their start and end apart: 1, of which 1 were waited for; matrix products, arithmetic and copies ran while one was open for 1% of the time, Pallas kernels for 0%

commit v1 on v0

v1 whole, which is shorter than its diff:
```python
import functools
import math

import jax
import jax.numpy as jnp
import numpy as np
from jax import lax
from jax.experimental import pallas as pl
from jax.experimental.pallas import tpu as pltpu
from jax.sharding import PartitionSpec as P

core_sq = 0.25
step_size = 1.0
block_size = 128
CAP = 2
feature_rows = 32
weight_rows = 16
chunk_blocks = 8
MESH = pl.DeviceIdType.MESH


def radau_matrix():
    sqrt_six = math.sqrt(6.0)
    return np.array(
        [
            [
                (88.0 - 7.0 * sqrt_six) / 360.0,
                (296.0 - 169.0 * sqrt_six) / 1800.0,
                (-2.0 + 3.0 * sqrt_six) / 225.0,
            ],
            [
                (296.0 + 169.0 * sqrt_six) / 1800.0,
                (88.0 + 7.0 * sqrt_six) / 360.0,
                (-2.0 - 3.0 * sqrt_six) / 225.0,
            ],
            [(16.0 - sqrt_six) / 36.0, (16.0 + sqrt_six) / 36.0, 1.0 / 9.0],
        ]
    )


def cut(value):
    head = value.astype(jnp.bfloat16).astype(jnp.float32)
    return head, value - head


def cut_thrice(value):
    high, rest = cut(value)
    middle, low = cut(rest)
    return high, middle, low


def cross(former, latter):
    return jnp.concatenate(
        [
            former[1:2] * latter[2:3] - former[2:3] * latter[1:2],
            former[2:3] * latter[0:1] - former[0:1] * latter[2:3],
            former[0:1] * latter[1:2] - former[1:2] * latter[0:1],
        ],
        axis=0,
    )


def features(pos):
    high, middle, low = cut_thrice(pos)
    square = jnp.sum(pos * pos, axis=0, keepdims=True)
    ones = jnp.ones((3, pos.shape[1]), jnp.float32)
    rest = jnp.zeros((feature_rows - 24, pos.shape[1]), jnp.float32)
    as_target = [high, high, middle, middle, high, low, ones, *cut_thrice(square), rest]
    as_source = [
        high * -2.0,
        middle * -2.0,
        high * -2.0,
        middle * -2.0,
        low * -2.0,
        high * -2.0,
        *cut_thrice(square + core_sq),
        ones,
        rest,
    ]
    return jnp.concatenate(as_target, axis=0), jnp.concatenate(as_source, axis=0)


def source_weights(pos, strength):
    weights = jnp.concatenate([strength, cross(pos, strength)], axis=0)
    high, low = cut(weights)
    rest = jnp.zeros((weight_rows - 12, pos.shape[1]), jnp.float32)
    return jnp.concatenate([high, low, rest], axis=0)


def kernel(
    n_tm,
    groups,
    table_q,
    small_ref,
    lists_ref,
    x_ref,
    a_ref,
    start_ref,
    live_ref,
    o_ref,
    own,
    stage,
    landed,
    table,
    targets,
    totals,
    inc_out,
    inc_in,
    send_sem,
    recv_sem,
    inc_send_sem,
    inc_recv_sem,
):
    tm, me = lax.axis_index("tm"), lax.axis_index("space")
    columns = x_ref.shape[1]
    blocks = columns // block_size
    list_len = lists_ref.shape[0] // blocks
    n_chunks = blocks // chunk_blocks
    chunk = chunk_blocks * block_size

    barrier = pltpu.get_barrier_semaphore()
    for d in range(1, groups):
        peer = lax.rem(me + d, groups)
        pl.semaphore_signal(barrier, inc=1, device_id=(tm, peer), device_id_type=MESH)
    for d in range(1, n_tm):
        peer = lax.rem(tm + d, n_tm)
        pl.semaphore_signal(barrier, inc=1, device_id=(peer, me), device_id_type=MESH)

    def block_at(index):
        return pl.ds(pl.multiple_of(index * block_size, block_size), block_size)

    for block in range(blocks):
        lanes = slice(block * block_size, (block + 1) * block_size)
        own[block, 0:9] = x_ref[:, lanes]
        own[block, 9:12] = a_ref[:, lanes]
    for d in range(1, groups):
        peer = lax.rem(me + d, groups)
        for k in range(CAP):
            lanes = slice(k * block_size, (k + 1) * block_size)
            stage[d, :, lanes] = own[small_ref[k * groups + peer]]

    pl.semaphore_wait(barrier, groups - 1 + n_tm - 1)

    def sources_copy(d):
        return pltpu.make_async_remote_copy(
            src_ref=stage.at[d],
            dst_ref=landed.at[d],
            send_sem=send_sem.at[d],
            recv_sem=recv_sem.at[d],
            device_id=(tm, lax.rem(me + d, groups)),
            device_id_type=MESH,
        )

    for d in range(1, groups):
        sources_copy(d).start()

    centre = jnp.sum(x_ref[...], axis=1, keepdims=True) * (1.0 / columns)

    def enter(slot, count, pos, strength, node):
        as_target, as_source = features(pos)
        weights = source_weights(pos, strength)
        rows = jnp.concatenate([as_source, weights], axis=0).astype(jnp.bfloat16)
        for k in range(count):
            table[slot + k, node] = rows[:, k * block_size : (k + 1) * block_size]
        return as_target

    own_step = 4

    def enter_own(step, carry):
        span = pl.ds(
            pl.multiple_of(step * own_step * block_size, block_size), own_step * block_size
        )
        for node in range(3):
            rows = slice(3 * node, 3 * node + 3)
            pos = x_ref[rows, span] - centre[rows]
            targets[node, :, span] = enter(
                step * own_step, own_step, pos, a_ref[:, span], node
            )
        return carry

    lax.fori_loop(0, blocks // own_step, enter_own, 0)

    for d in range(1, groups):
        sources_copy(d).wait()

    def enter_landed(step, carry):
        for node in range(3):
            rows = slice(3 * node, 3 * node + 3)
            pos = landed[step, rows, :] - centre[rows]
            slot = blocks + (step - 1) * CAP
            enter(slot, CAP, pos, landed[step, 9:12, :], node)
        return carry

    lax.fori_loop(1, groups, enter_landed, 0)

    def inc_copy(d, part):
        return pltpu.make_async_remote_copy(
            src_ref=inc_out.at[part],
            dst_ref=inc_in.at[d, part],
            send_sem=inc_send_sem.at[d, part],
            recv_sem=inc_recv_sem.at[d, part],
            device_id=(lax.rem(tm + d, n_tm), me),
            device_id_type=MESH,
        )

    def one_block(block, carry):
        slots = [lists_ref[block * list_len + j] for j in range(list_len)]
        here = block_at(block)
        for node in range(3):
            lhs = targets[node, :, here].T.astype(jnp.bfloat16)
            total = jnp.zeros((2 * block_size, weight_rows), jnp.float32)
            for j in range(0, list_len, 2):
                pair = jnp.concatenate(
                    [table[slots[j], node], table[slots[j + 1], node]], axis=1
                )
                distance = jnp.dot(
                    lhs, pair[:feature_rows], preferred_element_type=jnp.float32
                )
                inverse = lax.rsqrt(distance)
                value = inverse * inverse * inverse
                high = value.astype(jnp.bfloat16)
                low = (value - high.astype(jnp.float32)).astype(jnp.bfloat16)
                total += lax.dot_general(
                    jnp.concatenate([high, low], axis=0),
                    pair[feature_rows:],
                    (((1,), (1,)), ((), ())),
                    preferred_element_type=jnp.float32,
                )
            total = total[:block_size] + total[block_size:]
            totals[node, :, here] = total.T
        return carry

    def one_chunk(part, carry):
        lax.fori_loop(part * chunk_blocks, (part + 1) * chunk_blocks, one_block, 0)
        span = pl.ds(pl.multiple_of(part * chunk, block_size), chunk)
        scale = live_ref[:, span] * (-0.25 / math.pi)
        rates = []
        for node in range(3):
            rows = slice(3 * node, 3 * node + 3)
            pos = x_ref[rows, span] - centre[rows]
            sums = totals[node, :, span]
            spread = cross(pos, sums[0:3] + sums[6:9]) - (sums[3:6] + sums[9:12])
            rates.append(spread * scale)
        start = start_ref[:, span]
        for node in range(3):
            quadrature = step_size * (
                table_q[node][0] * rates[0]
                + table_q[node][1] * rates[1]
                + table_q[node][2] * rates[2]
            )
            o_ref[3 * node : 3 * node + 3, span] = start + quadrature
        inc_out[part] = quadrature
        for d in range(1, n_tm):

            @pl.when(tm + d < n_tm)
            def _():
                inc_copy(d, part).start()

        return carry

    lax.fori_loop(0, n_chunks, one_chunk, 0)

    def finish(part, carry):
        span = pl.ds(pl.multiple_of(part * chunk, block_size), chunk)
        for d in range(1, n_tm):

            @pl.when(tm + d < n_tm)
            def _():
                inc_copy(d, part).wait_send()

            @pl.when(tm - d >= 0)
            def _():
                inc_copy(d, part).wait_recv()
                arrived = inc_in[d, part]
                for node in range(3):
                    rows = slice(3 * node, 3 * node + 3)
                    o_ref[rows, span] = o_ref[rows, span] + arrived

        return carry

    lax.fori_loop(0, n_chunks, finish, 0)


def shards(node_states, strengths, start_state, lists, counts):
    n_tm, groups = lax.axis_size("tm"), lax.axis_size("space")
    me = lax.axis_index("space")
    blocks = lists.shape[0] // groups
    columns = node_states.shape[2]
    n_chunks = blocks // chunk_blocks
    slots = blocks + (groups - 1) * CAP

    by_shard = lists.reshape(groups, -1)
    owner = by_shard // blocks
    local = by_shard - me * blocks
    asked = owner == me
    first = jnp.min(jnp.where(asked, local, blocks - 1), axis=1)
    last = jnp.max(jnp.where(asked, local, 0), axis=1)
    my_lists = lax.dynamic_index_in_dim(by_shard, me, 0, keepdims=False)
    shard_ids = jnp.arange(groups, dtype=jnp.int32)[:, None]
    lowest = jnp.min(
        jnp.where(my_lists[None] // blocks == shard_ids, my_lists[None], lists.shape[0]), axis=1
    )
    small = jnp.concatenate([first, last])
    shard = my_lists // blocks
    low = jnp.sum(jnp.where(shard[None] == shard_ids, lowest[:, None], 0), axis=0)
    away = (me - shard + groups) % groups
    my_slots = jnp.where(
        shard == me,
        my_lists - me * blocks,
        blocks + (away - 1) * CAP + (my_lists != low).astype(jnp.int32),
    )
    live_count = lax.dynamic_index_in_dim(counts, me, 0, keepdims=False)
    live = jnp.arange(columns, dtype=jnp.int32)[None] < live_count * block_size

    chunk = chunk_blocks * block_size
    out = pl.pallas_call(
        functools.partial(kernel, n_tm, groups, radau_matrix().tolist()),
        out_shape=jax.ShapeDtypeStruct((9, columns), jnp.float32),
        in_specs=[pl.BlockSpec(memory_space=pltpu.SMEM)] * 2
        + [pl.BlockSpec(memory_space=pltpu.VMEM)] * 4,
        out_specs=pl.BlockSpec(memory_space=pltpu.VMEM),
        scratch_shapes=[
            pltpu.VMEM((blocks, 12, block_size), jnp.float32),
            pltpu.VMEM((groups, 12, CAP * block_size), jnp.float32),
            pltpu.VMEM((groups, 12, CAP * block_size), jnp.float32),
            pltpu.VMEM((slots, 3, feature_rows + weight_rows, block_size), jnp.bfloat16),
            pltpu.VMEM((3, feature_rows, columns), jnp.float32),
            pltpu.VMEM((3, weight_rows, columns), jnp.float32),
            pltpu.VMEM((n_chunks, 3, chunk), jnp.float32),
            pltpu.VMEM((n_tm, n_chunks, 3, chunk), jnp.float32),
            pltpu.SemaphoreType.DMA((groups,)),
            pltpu.SemaphoreType.DMA((groups,)),
            pltpu.SemaphoreType.DMA((n_tm, n_chunks)),
            pltpu.SemaphoreType.DMA((n_tm, n_chunks)),
        ],
        compiler_params=pltpu.CompilerParams(
            collective_id=0, has_side_effects=True, vmem_limit_bytes=40 << 20
        ),
        name="vortex_window",
    )(small, my_slots, node_states[0], strengths, start_state, live.astype(jnp.float32))
    return out.reshape(1, 9, -1)


def solution(mesh):
    return jax.shard_map(
        shards,
        mesh=mesh,
        in_specs=(P("tm", None, "space"), P(None, "space"), P(None, "space"), P(), P()),
        out_specs=P("tm", None, "space"),
        check_vma=False,
    )
```

time: 249 us -> 72.8 us (0.29)
  other arithmetic: 82.9 us -> 0.64 us
  matrix products: 67.8 us -> 0 us
  Pallas kernels: 0 us -> 67.5 us
  waiting for transfers between devices: 45.3 us -> 0 us
  local copies, waits for them, and re-layouts: 30.9 us -> 3.72 us
  between operations: 13.5 us -> 0.7 us
  blocking collectives: 5.79 us -> 0 us
    reduce_sum x16 -> x1, other arithmetic: 75.5 us -> 0.09 us  [shards(): jnp.sum(jnp.where(shard[None] == shard_ids, lowest[:, None], 0), axis=0)]
    dot_general x17 -> x0, matrix products: 67.8 us -> none  [the longest x16 67.3 us: block_velocity(): jnp.einsum('mks,msb->mkb', weights, kernel, precision=lax.Precision.HIGHEST)]
    pallas_call x0 -> x1, Pallas kernels: none -> 67.5 us  [shards(): pl.pallas_call(functools.partial(kernel, n_tm, groups, radau_matrix().tol...]
    all_gather x1 -> x0, waiting for transfers between devices: 45.3 us -> none  [shards(): source_table = lax.all_gather(own_blocks, 'space', axis=0, tiled=True)]
    dynamic_slice x19 -> x1, local copies, waits for them, and re-layouts: 12.8 us -> 1.25 us  [shards(): live_count = lax.dynamic_index_in_dim(counts, me, 0, keepdims=False)]
    gather x16 -> x0, local copies, waits for them, and re-layouts: 9.21 us -> none  [one_group(): group_sources = jnp.take(source_table, group_slots.reshape(-1), axis=0)]
    all_gather x1 -> x0, blocking collectives: 5.79 us -> none  [entering(): pieces = lax.all_gather(value, axis)]
    reshape x66 -> x2, local copies, waits for them, and re-layouts: 4.21 us -> 0.93 us  [the longest x1 0.81 us: shards(): return out.reshape(1, 9, -1)]
  transfers between devices with their start and end apart: 1 -> 0, of which waited for: 1 -> 0; matrix products, arithmetic and copies ran while one was open for 1% -> 0% of each run, Pallas kernels for 0% -> 0%
where the time goes in v1:
time: 72.8 us; the launch traced here: 72.6 us
  Pallas kernels  67.5 us (93%)
  local copies, waits for them, and re-layouts  3.72 us (5%)
    pallas_call x1, Pallas kernels, shards(): pl.pallas_call(functools.partial(kernel, n_tm, groups, radau_matrix().tol...  67.5 us

profile of v1, /device:TPU:0, one launch (start us, length us, event | category | flops | bytes accessed | tf_op | source)
XLA Modules:
  0.0 72.6 jit_solution(10636090144093878482)
XLA Ops:
  0.0 0.0 copy-start.3
  0.0 1.2 %dynamic_slice.9 = s32[1]{0:T(128)} dynamic-slice(s32[8]{0:T(128)} %param.9, s32[]{:T(128)S(6)} %select_n.54), dynamic_slice_sizes={1} | dynamic-slice | bytes 12 | tf_op jit(solution)/shard_map/jit(dynamic_index_in_dim)/dynamic_slice | solution.py:312
  1.9 0.0 copy-done.3
  2.0 0.1 reduce_min.26
  2.0 0.1 reduce_min.27
  2.2 0.1 reduce_max.14
  2.2 0.1 reduce_max.18
  2.4 0.1 pad_add_fusion.small_ref
  2.5 0.0 copy-start.2
  2.5 0.1 copy.9
  2.6 0.1 reshape.23
  2.7 0.1 select_reduce_fusion.3
  2.9 0.1 select_reduce_fusion.2
  3.0 0.4 copy-done.2
  3.4 0.0 copy-start
  3.4 0.0 copy-start.1
  3.4 0.1 copy.13
  3.5 0.7 %copy-done = f32[3,4096]{1,0:T(4,128)S(1)} copy-done((f32[3,4096]{1,0:T(4,128)S(1)}, f32[3,4096]{1,0:T(4,128)}, u32[]{:S(2)}) %copy-start) | copy-done | bytes 49176
  4.2 0.0 copy-done.1
  4.2 67.5 %vortex_window.1 = f32[9,4096]{1,0:T(8,128)S(1)} custom-call(s32[16]{0:T(128)S(1)} %pad_add_fusion.small_ref, s32[384]{0:T(512)S(1)} %fusion.9.lists_ref, f32[9,4096]{1,0:T(8,128)S(1)} %bitcast.6, f32[3,4096]{1,0:T(4,128)S(1)} %copy-done, f32[3,4096]{1,0:T(4,128)S(1)} %copy-done.1, f32[1,4096]{1,0:T(1,128)S(1)} %compare_convert_fusion.live_ref), custom_call_target="tpu_custom_call" | custom-call | tf_op jit(solution)/shard_map/vortex_window/pallas_call | solution.py:316
  71.8 0.8 %copy.10 = f32[1,9,4096]{2,0,1:T(1,128)} copy(f32[1,9,4096]{2,1,0:T(8,128)S(1)} %bitcast.5) | data formatting | bytes 294912 | tf_op jit(solution)/shard_map/reshape | solution.py:341
  (4 shorter events, 0.1 us)
Async XLA Ops:
  0.0 1.9 %copy-start.3 = (s32[256,12]{0,1:T(8,128)S(1)}, s32[256,12]{0,1:T(8,128)}, u32[]{:S(2)}) copy-start(s32[256,12]{0,1:T(8,128)} %param.8) | copy-start | bytes 36868
  2.5 0.9 %copy-start.2 = (f32[1,9,4096]{2,0,1:T(1,128)S(1)}, f32[1,9,4096]{2,0,1:T(1,128)}, u32[]{:S(2)}) copy-start(f32[1,9,4096]{2,0,1:T(1,128)} %param.5) | copy-start | bytes 442372
  3.4 0.8 %copy-start = (f32[3,4096]{1,0:T(4,128)S(1)}, f32[3,4096]{1,0:T(4,128)}, u32[]{:S(2)}) copy-start(f32[3,4096]{1,0:T(4,128)} %a_ref.1) | copy-start | bytes 147460
  3.4 0.9 %copy-start.1 = (f32[3,4096]{1,0:T(4,128)S(1)}, f32[3,4096]{1,0:T(4,128)}, u32[]{:S(2)}) copy-start(f32[3,4096]{1,0:T(4,128)} %start_ref.1) | copy-start | bytes 147460

commit v2 on v1

--- a/solution.py
+++ b/solution.py
@@ -103,6 +103,7 @@
     landed,
     table,
     targets,
+    parts,
     totals,
     inc_out,
     inc_in,
@@ -208,7 +209,7 @@
         here = block_at(block)
         for node in range(3):
             lhs = targets[node, :, here].T.astype(jnp.bfloat16)
-            total = jnp.zeros((2 * block_size, weight_rows), jnp.float32)
+            weights = []
             for j in range(0, list_len, 2):
                 pair = jnp.concatenate(
                     [table[slots[j], node], table[slots[j + 1], node]], axis=1
@@ -220,12 +221,16 @@
                 value = inverse * inverse * inverse
                 high = value.astype(jnp.bfloat16)
                 low = (value - high.astype(jnp.float32)).astype(jnp.bfloat16)
-                total += lax.dot_general(
-                    jnp.concatenate([high, low], axis=0),
-                    pair[feature_rows:],
-                    (((1,), (1,)), ((), ())),
-                    preferred_element_type=jnp.float32,
-                )
+                lanes = slice(j * block_size, (j + 2) * block_size)
+                parts[node, :block_size, lanes] = high
+                parts[node, block_size:, lanes] = low
+                weights.append(pair[feature_rows:])
+            total = lax.dot_general(
+                parts[node],
+                jnp.concatenate(weights, axis=1),
+                (((1,), (1,)), ((), ())),
+                preferred_element_type=jnp.float32,
+            )
             total = total[:block_size] + total[block_size:]
             totals[node, :, here] = total.T
         return carry
@@ -325,6 +330,7 @@
             pltpu.VMEM((groups, 12, CAP * block_size), jnp.float32),
             pltpu.VMEM((slots, 3, feature_rows + weight_rows, block_size), jnp.bfloat16),
             pltpu.VMEM((3, feature_rows, columns), jnp.float32),
+            pltpu.VMEM((3, 2 * block_size, lists.shape[1] * block_size), jnp.bfloat16),
             pltpu.VMEM((3, weight_rows, columns), jnp.float32),
             pltpu.VMEM((n_chunks, 3, chunk), jnp.float32),
             pltpu.VMEM((n_tm, n_chunks, 3, chunk), jnp.float32),

time: 72.8 us -> 58.3 us (0.80)
  Pallas kernels: 67.5 us -> 53 us
    pallas_call x1, Pallas kernels: 67.5 us -> 53 us  [shards(): pl.pallas_call(functools.partial(kernel, n_tm, groups, radau_matrix().tol...]
where the time goes in v2:
time: 58.3 us; the launch traced here: 58.1 us
  Pallas kernels  53 us (91%)
  local copies, waits for them, and re-layouts  3.72 us (6%)
  between operations  0.7 us (1%)
  other arithmetic  0.64 us (1%)
    pallas_call x1, Pallas kernels, shards(): pl.pallas_call(functools.partial(kernel, n_tm, groups, radau_matrix().tol...  53 us
    unnamed x10, local copies, waits for them, and re-layouts  1.39 us
    dynamic_slice x1, local copies, waits for them, and re-layouts, shards(): live_count = lax.dynamic_index_in_dim(counts, me, 0, keepdims=False)  1.25 us

profile of v2, /device:TPU:0, one launch (start us, length us, event | category | flops | bytes accessed | tf_op | source)
XLA Modules:
  0.0 58.1 jit_solution(17302015314273686074)
XLA Ops:
  0.0 0.0 copy-start.3
  0.0 1.2 %dynamic_slice.9 = s32[1]{0:T(128)} dynamic-slice(s32[8]{0:T(128)} %param.9, s32[]{:T(128)S(6)} %select_n.54), dynamic_slice_sizes={1} | dynamic-slice | bytes 12 | tf_op jit(solution)/shard_map/jit(dynamic_index_in_dim)/dynamic_slice | solution.py:317
  1.9 0.0 copy-done.3
  2.0 0.1 reduce_min.26
  2.0 0.1 reduce_min.27
  2.2 0.1 reduce_max.14
  2.2 0.1 reduce_max.18
  2.4 0.1 pad_add_fusion.small_ref
  2.5 0.0 copy-start.2
  2.5 0.1 copy.9
  2.6 0.1 reshape.23
  2.7 0.1 select_reduce_fusion.3
  2.9 0.1 select_reduce_fusion.2
  3.0 0.4 copy-done.2
  3.4 0.0 copy-start
  3.4 0.0 copy-start.1
  3.4 0.1 copy.13
  3.5 0.7 %copy-done = f32[3,4096]{1,0:T(4,128)S(1)} copy-done((f32[3,4096]{1,0:T(4,128)S(1)}, f32[3,4096]{1,0:T(4,128)}, u32[]{:S(2)}) %copy-start) | copy-done | bytes 49176
  4.2 0.0 copy-done.1
  4.2 53.0 %vortex_window.1 = f32[9,4096]{1,0:T(8,128)S(1)} custom-call(s32[16]{0:T(128)S(1)} %pad_add_fusion.small_ref, s32[384]{0:T(512)S(1)} %fusion.9.lists_ref, f32[9,4096]{1,0:T(8,128)S(1)} %bitcast.6, f32[3,4096]{1,0:T(4,128)S(1)} %copy-done, f32[3,4096]{1,0:T(4,128)S(1)} %copy-done.1, f32[1,4096]{1,0:T(1,128)S(1)} %compare_convert_fusion.live_ref), custom_call_target="tpu_custom_call" | custom-call | tf_op jit(solution)/shard_map/vortex_window/pallas_call | solution.py:321
  57.2 0.8 %copy.10 = f32[1,9,4096]{2,0,1:T(1,128)} copy(f32[1,9,4096]{2,1,0:T(8,128)S(1)} %bitcast.5) | data formatting | bytes 294912 | tf_op jit(solution)/shard_map/reshape | solution.py:347
  (4 shorter events, 0.1 us)
Async XLA Ops:
  0.0 1.9 %copy-start.3 = (s32[256,12]{0,1:T(8,128)S(1)}, s32[256,12]{0,1:T(8,128)}, u32[]{:S(2)}) copy-start(s32[256,12]{0,1:T(8,128)} %param.8) | copy-start | bytes 36868
  2.5 0.9 %copy-start.2 = (f32[1,9,4096]{2,0,1:T(1,128)S(1)}, f32[1,9,4096]{2,0,1:T(1,128)}, u32[]{:S(2)}) copy-start(f32[1,9,4096]{2,0,1:T(1,128)} %param.5) | copy-start | bytes 442372
  3.4 0.8 %copy-start = (f32[3,4096]{1,0:T(4,128)S(1)}, f32[3,4096]{1,0:T(4,128)}, u32[]{:S(2)}) copy-start(f32[3,4096]{1,0:T(4,128)} %a_ref.1) | copy-start | bytes 147460
  3.4 0.9 %copy-start.1 = (f32[3,4096]{1,0:T(4,128)S(1)}, f32[3,4096]{1,0:T(4,128)}, u32[]{:S(2)}) copy-start(f32[3,4096]{1,0:T(4,128)} %start_ref.1) | copy-start | bytes 147460

commit v3 on v1

--- a/solution.py
+++ b/solution.py
@@ -103,6 +103,7 @@
     landed,
     table,
     targets,
+    parts,
     totals,
     inc_out,
     inc_in,
@@ -156,13 +157,15 @@
 
     centre = jnp.sum(x_ref[...], axis=1, keepdims=True) * (1.0 / columns)
 
-    def enter(slot, count, pos, strength, node):
-        as_target, as_source = features(pos)
-        weights = source_weights(pos, strength)
-        rows = jnp.concatenate([as_source, weights], axis=0).astype(jnp.bfloat16)
+    def enter(slot, count, pos, strength):
+        here = [pos[3 * node : 3 * node + 3] for node in range(3)]
+        pairs = [features(place) for place in here]
+        weights = [source_weights(place, strength) for place in here]
+        rows = [as_source for _, as_source in pairs] + weights
+        rows = jnp.concatenate(rows, axis=0).astype(jnp.bfloat16)
         for k in range(count):
-            table[slot + k, node] = rows[:, k * block_size : (k + 1) * block_size]
-        return as_target
+            table[slot + k] = rows[:, k * block_size : (k + 1) * block_size]
+        return jnp.concatenate([as_target for as_target, _ in pairs], axis=0)
 
     own_step = 4
 
@@ -170,12 +173,8 @@
         span = pl.ds(
             pl.multiple_of(step * own_step * block_size, block_size), own_step * block_size
         )
-        for node in range(3):
-            rows = slice(3 * node, 3 * node + 3)
-            pos = x_ref[rows, span] - centre[rows]
-            targets[node, :, span] = enter(
-                step * own_step, own_step, pos, a_ref[:, span], node
-            )
+        pos = x_ref[:, span] - centre
+        targets[:, span] = enter(step * own_step, own_step, pos, a_ref[:, span])
         return carry
 
     lax.fori_loop(0, blocks // own_step, enter_own, 0)
@@ -184,11 +183,8 @@
         sources_copy(d).wait()
 
     def enter_landed(step, carry):
-        for node in range(3):
-            rows = slice(3 * node, 3 * node + 3)
-            pos = landed[step, rows, :] - centre[rows]
-            slot = blocks + (step - 1) * CAP
-            enter(slot, CAP, pos, landed[step, 9:12, :], node)
+        pos = landed[step, 0:9, :] - centre
+        enter(blocks + (step - 1) * CAP, CAP, pos, landed[step, 9:12, :])
         return carry
 
     lax.fori_loop(1, groups, enter_landed, 0)
@@ -206,28 +202,37 @@
     def one_block(block, carry):
         slots = [lists_ref[block * list_len + j] for j in range(list_len)]
         here = block_at(block)
+        turned = targets[:, here].T
+        node_of = lax.broadcasted_iota(jnp.int32, turned.shape, 1) // feature_rows
+        lhs = [jnp.where(node_of == node, turned, 0.0) for node in range(3)]
+        lhs = jnp.concatenate(lhs, axis=0).astype(jnp.bfloat16)
+        weights = []
+        for j in range(0, list_len, 2):
+            pair = jnp.concatenate([table[slots[j]], table[slots[j + 1]]], axis=1)
+            distance = jnp.dot(
+                lhs, pair[: 3 * feature_rows], preferred_element_type=jnp.float32
+            )
+            inverse = lax.rsqrt(distance)
+            value = inverse * inverse * inverse
+            high = value.astype(jnp.bfloat16)
+            low = (value - high.astype(jnp.float32)).astype(jnp.bfloat16)
+            lanes = slice(j * block_size, (j + 2) * block_size)
+            parts[: 3 * block_size, lanes] = high
+            parts[3 * block_size :, lanes] = low
+            weights.append(pair[3 * feature_rows :])
+        total = lax.dot_general(
+            parts[...],
+            jnp.concatenate(weights, axis=1),
+            (((1,), (1,)), ((), ())),
+            preferred_element_type=jnp.float32,
+        )
+        total = total[: 3 * block_size] + total[3 * block_size :]
+        node_of = lax.broadcasted_iota(jnp.int32, (block_size, 3 * weight_rows), 1) // weight_rows
+        kept = jnp.zeros((block_size, 3 * weight_rows), jnp.float32)
         for node in range(3):
-            lhs = targets[node, :, here].T.astype(jnp.bfloat16)
-            total = jnp.zeros((2 * block_size, weight_rows), jnp.float32)
-            for j in range(0, list_len, 2):
-                pair = jnp.concatenate(
-                    [table[slots[j], node], table[slots[j + 1], node]], axis=1
-                )
-                distance = jnp.dot(
-                    lhs, pair[:feature_rows], preferred_element_type=jnp.float32
-                )
-                inverse = lax.rsqrt(distance)
-                value = inverse * inverse * inverse
-                high = value.astype(jnp.bfloat16)
-                low = (value - high.astype(jnp.float32)).astype(jnp.bfloat16)
-                total += lax.dot_general(
-                    jnp.concatenate([high, low], axis=0),
-                    pair[feature_rows:],
-                    (((1,), (1,)), ((), ())),
-                    preferred_element_type=jnp.float32,
-                )
-            total = total[:block_size] + total[block_size:]
-            totals[node, :, here] = total.T
+            rows = total[node * block_size : (node + 1) * block_size]
+            kept = jnp.where(node_of == node, rows, kept)
+        totals[:, here] = kept.T
         return carry
 
     def one_chunk(part, carry):
@@ -238,7 +243,7 @@
         for node in range(3):
             rows = slice(3 * node, 3 * node + 3)
             pos = x_ref[rows, span] - centre[rows]
-            sums = totals[node, :, span]
+            sums = totals[weight_rows * node : weight_rows * (node + 1), span]
             spread = cross(pos, sums[0:3] + sums[6:9]) - (sums[3:6] + sums[9:12])
             rates.append(spread * scale)
         start = start_ref[:, span]
@@ -323,9 +328,10 @@
             pltpu.VMEM((blocks, 12, block_size), jnp.float32),
             pltpu.VMEM((groups, 12, CAP * block_size), jnp.float32),
             pltpu.VMEM((groups, 12, CAP * block_size), jnp.float32),
-            pltpu.VMEM((slots, 3, feature_rows + weight_rows, block_size), jnp.bfloat16),
-            pltpu.VMEM((3, feature_rows, columns), jnp.float32),
-            pltpu.VMEM((3, weight_rows, columns), jnp.float32),
+            pltpu.VMEM((slots, 3 * (feature_rows + weight_rows), block_size), jnp.bfloat16),
+            pltpu.VMEM((3 * feature_rows, columns), jnp.float32),
+            pltpu.VMEM((6 * block_size, lists.shape[1] * block_size), jnp.bfloat16),
+            pltpu.VMEM((3 * weight_rows, columns), jnp.float32),
             pltpu.VMEM((n_chunks, 3, chunk), jnp.float32),
             pltpu.VMEM((n_tm, n_chunks, 3, chunk), jnp.float32),
             pltpu.SemaphoreType.DMA((groups,)),

time: 72.8 us -> 55.8 us (0.77)
  Pallas kernels: 67.5 us -> 50.5 us
    pallas_call x1, Pallas kernels: 67.5 us -> 50.5 us  [shards(): pl.pallas_call(functools.partial(kernel, n_tm, groups, radau_matrix().tol...]
where the time goes in v3:
time: 55.8 us; the launch traced here: 55.6 us
  Pallas kernels  50.5 us (91%)
  local copies, waits for them, and re-layouts  3.72 us (7%)
  between operations  0.7 us (1%)
  other arithmetic  0.64 us (1%)
    pallas_call x1, Pallas kernels, shards(): pl.pallas_call(functools.partial(kernel, n_tm, groups, radau_matrix().tol...  50.5 us
    unnamed x10, local copies, waits for them, and re-layouts  1.39 us
    dynamic_slice x1, local copies, waits for them, and re-layouts, shards(): live_count = lax.dynamic_index_in_dim(counts, me, 0, keepdims=False)  1.25 us

profile of v3, /device:TPU:0, one launch (start us, length us, event | category | flops | bytes accessed | tf_op | source)
XLA Modules:
  0.0 55.6 jit_solution(10298345108293785365)
XLA Ops:
  0.0 0.0 copy-start.3
  0.0 1.2 %dynamic_slice.9 = s32[1]{0:T(128)} dynamic-slice(s32[8]{0:T(128)} %param.9, s32[]{:T(128)S(6)} %select_n.54), dynamic_slice_sizes={1} | dynamic-slice | bytes 12 | tf_op jit(solution)/shard_map/jit(dynamic_index_in_dim)/dynamic_slice | solution.py:317
  1.9 0.0 copy-done.3
  2.0 0.1 reduce_min.26
  2.0 0.1 reduce_min.27
  2.2 0.1 reduce_max.14
  2.2 0.1 reduce_max.18
  2.4 0.1 pad_add_fusion.small_ref
  2.5 0.0 copy-start.2
  2.5 0.1 copy.9
  2.6 0.1 reshape.23
  2.7 0.1 select_reduce_fusion.3
  2.9 0.1 select_reduce_fusion.2
  3.0 0.4 copy-done.2
  3.4 0.0 copy-start
  3.4 0.0 copy-start.1
  3.4 0.1 copy.13
  3.5 0.7 %copy-done = f32[3,4096]{1,0:T(4,128)S(1)} copy-done((f32[3,4096]{1,0:T(4,128)S(1)}, f32[3,4096]{1,0:T(4,128)}, u32[]{:S(2)}) %copy-start) | copy-done | bytes 49176
  4.2 0.0 copy-done.1
  4.2 50.5 %vortex_window.1 = f32[9,4096]{1,0:T(8,128)S(1)} custom-call(s32[16]{0:T(128)S(1)} %pad_add_fusion.small_ref, s32[384]{0:T(512)S(1)} %fusion.9.lists_ref, f32[9,4096]{1,0:T(8,128)S(1)} %bitcast.6, f32[3,4096]{1,0:T(4,128)S(1)} %copy-done, f32[3,4096]{1,0:T(4,128)S(1)} %copy-done.1, f32[1,4096]{1,0:T(1,128)S(1)} %compare_convert_fusion.live_ref), custom_call_target="tpu_custom_call" | custom-call | tf_op jit(solution)/shard_map/vortex_window/pallas_call | solution.py:321
  54.8 0.8 %copy.10 = f32[1,9,4096]{2,0,1:T(1,128)} copy(f32[1,9,4096]{2,1,0:T(8,128)S(1)} %bitcast.5) | data formatting | bytes 294912 | tf_op jit(solution)/shard_map/reshape | solution.py:347
  (4 shorter events, 0.1 us)
Async XLA Ops:
  0.0 1.9 %copy-start.3 = (s32[256,12]{0,1:T(8,128)S(1)}, s32[256,12]{0,1:T(8,128)}, u32[]{:S(2)}) copy-start(s32[256,12]{0,1:T(8,128)} %param.8) | copy-start | bytes 36868
  2.5 0.9 %copy-start.2 = (f32[1,9,4096]{2,0,1:T(1,128)S(1)}, f32[1,9,4096]{2,0,1:T(1,128)}, u32[]{:S(2)}) copy-start(f32[1,9,4096]{2,0,1:T(1,128)} %param.5) | copy-start | bytes 442372
  3.4 0.8 %copy-start = (f32[3,4096]{1,0:T(4,128)S(1)}, f32[3,4096]{1,0:T(4,128)}, u32[]{:S(2)}) copy-start(f32[3,4096]{1,0:T(4,128)} %a_ref.1) | copy-start | bytes 147460
  3.4 0.9 %copy-start.1 = (f32[3,4096]{1,0:T(4,128)S(1)}, f32[3,4096]{1,0:T(4,128)}, u32[]{:S(2)}) copy-start(f32[3,4096]{1,0:T(4,128)} %start_ref.1) | copy-start | bytes 147460

commit v4 on v3

--- a/solution.py
+++ b/solution.py
@@ -199,29 +199,32 @@
             device_id_type=MESH,
         )
 
-    def one_block(block, carry):
+    def interact(block, buffer):
         slots = [lists_ref[block * list_len + j] for j in range(list_len)]
         here = block_at(block)
         turned = targets[:, here].T
         node_of = lax.broadcasted_iota(jnp.int32, turned.shape, 1) // feature_rows
         lhs = [jnp.where(node_of == node, turned, 0.0) for node in range(3)]
         lhs = jnp.concatenate(lhs, axis=0).astype(jnp.bfloat16)
-        weights = []
         for j in range(0, list_len, 2):
-            pair = jnp.concatenate([table[slots[j]], table[slots[j + 1]]], axis=1)
+            pair = [table[slot, : 3 * feature_rows] for slot in slots[j : j + 2]]
             distance = jnp.dot(
-                lhs, pair[: 3 * feature_rows], preferred_element_type=jnp.float32
+                lhs, jnp.concatenate(pair, axis=1), preferred_element_type=jnp.float32
             )
             inverse = lax.rsqrt(distance)
             value = inverse * inverse * inverse
             high = value.astype(jnp.bfloat16)
             low = (value - high.astype(jnp.float32)).astype(jnp.bfloat16)
             lanes = slice(j * block_size, (j + 2) * block_size)
-            parts[: 3 * block_size, lanes] = high
-            parts[3 * block_size :, lanes] = low
-            weights.append(pair[3 * feature_rows :])
+            parts[buffer, : 3 * block_size, lanes] = high
+            parts[buffer, 3 * block_size :, lanes] = low
+
+    def weigh(block, buffer):
+        slots = [lists_ref[block * list_len + j] for j in range(list_len)]
+        here = block_at(block)
+        weights = [table[slot, 3 * feature_rows :] for slot in slots]
         total = lax.dot_general(
-            parts[...],
+            parts[buffer],
             jnp.concatenate(weights, axis=1),
             (((1,), (1,)), ((), ())),
             preferred_element_type=jnp.float32,
@@ -233,10 +236,17 @@
             rows = total[node * block_size : (node + 1) * block_size]
             kept = jnp.where(node_of == node, rows, kept)
         totals[:, here] = kept.T
+
+    def two_blocks(step, carry):
+        interact(2 * step + 1, 1)
+        weigh(2 * step, 0)
+        interact(jnp.minimum(2 * step + 2, blocks - 1), 0)
+        weigh(2 * step + 1, 1)
         return carry
 
     def one_chunk(part, carry):
-        lax.fori_loop(part * chunk_blocks, (part + 1) * chunk_blocks, one_block, 0)
+        steps = chunk_blocks // 2
+        lax.fori_loop(part * steps, (part + 1) * steps, two_blocks, 0)
         span = pl.ds(pl.multiple_of(part * chunk, block_size), chunk)
         scale = live_ref[:, span] * (-0.25 / math.pi)
         rates = []
@@ -263,6 +273,7 @@
 
         return carry
 
+    interact(0, 0)
     lax.fori_loop(0, n_chunks, one_chunk, 0)
 
     def finish(part, carry):
@@ -330,7 +341,7 @@
             pltpu.VMEM((groups, 12, CAP * block_size), jnp.float32),
             pltpu.VMEM((slots, 3 * (feature_rows + weight_rows), block_size), jnp.bfloat16),
             pltpu.VMEM((3 * feature_rows, columns), jnp.float32),
-            pltpu.VMEM((6 * block_size, lists.shape[1] * block_size), jnp.bfloat16),
+            pltpu.VMEM((2, 6 * block_size, lists.shape[1] * block_size), jnp.bfloat16),
             pltpu.VMEM((3 * weight_rows, columns), jnp.float32),
             pltpu.VMEM((n_chunks, 3, chunk), jnp.float32),
             pltpu.VMEM((n_tm, n_chunks, 3, chunk), jnp.float32),

time: 55.8 us -> 55.6 us (level)
  no operation moved by 1% of the time
where the time goes in v4:
time: 55.6 us; the launch traced here: 55.4 us
  Pallas kernels  50.3 us (90%)
  local copies, waits for them, and re-layouts  3.72 us (7%)
  between operations  0.7 us (1%)
  other arithmetic  0.64 us (1%)
    pallas_call x1, Pallas kernels, shards(): pl.pallas_call(functools.partial(kernel, n_tm, groups, radau_matrix().tol...  50.3 us
    unnamed x10, local copies, waits for them, and re-layouts  1.39 us
    dynamic_slice x1, local copies, waits for them, and re-layouts, shards(): live_count = lax.dynamic_index_in_dim(counts, me, 0, keepdims=False)  1.25 us

profile of v4, /device:TPU:0, one launch (start us, length us, event | category | flops | bytes accessed | tf_op | source)
XLA Modules:
  0.0 55.4 jit_solution(8761050115828279020)
XLA Ops:
  0.0 0.0 copy-start.3
  0.0 1.2 %dynamic_slice.9 = s32[1]{0:T(128)} dynamic-slice(s32[8]{0:T(128)} %param.9, s32[]{:T(128)S(6)} %select_n.54), dynamic_slice_sizes={1} | dynamic-slice | bytes 12 | tf_op jit(solution)/shard_map/jit(dynamic_index_in_dim)/dynamic_slice | solution.py:328
  1.9 0.0 copy-done.3
  2.0 0.1 reduce_min.26
  2.0 0.1 reduce_min.27
  2.2 0.1 reduce_max.14
  2.2 0.1 reduce_max.18
  2.4 0.1 pad_add_fusion.small_ref
  2.5 0.0 copy-start.2
  2.5 0.1 copy.9
  2.6 0.1 reshape.23
  2.7 0.1 select_reduce_fusion.3
  2.9 0.1 select_reduce_fusion.2
  3.0 0.4 copy-done.2
  3.4 0.0 copy-start
  3.4 0.0 copy-start.1
  3.4 0.1 copy.13
  3.5 0.7 %copy-done = f32[3,4096]{1,0:T(4,128)S(1)} copy-done((f32[3,4096]{1,0:T(4,128)S(1)}, f32[3,4096]{1,0:T(4,128)}, u32[]{:S(2)}) %copy-start) | copy-done | bytes 49176
  4.2 0.0 copy-done.1
  4.2 50.3 %vortex_window.1 = f32[9,4096]{1,0:T(8,128)S(1)} custom-call(s32[16]{0:T(128)S(1)} %pad_add_fusion.small_ref, s32[384]{0:T(512)S(1)} %fusion.9.lists_ref, f32[9,4096]{1,0:T(8,128)S(1)} %bitcast.6, f32[3,4096]{1,0:T(4,128)S(1)} %copy-done, f32[3,4096]{1,0:T(4,128)S(1)} %copy-done.1, f32[1,4096]{1,0:T(1,128)S(1)} %compare_convert_fusion.live_ref), custom_call_target="tpu_custom_call" | custom-call | tf_op jit(solution)/shard_map/vortex_window/pallas_call | solution.py:332
  54.6 0.8 %copy.10 = f32[1,9,4096]{2,0,1:T(1,128)} copy(f32[1,9,4096]{2,1,0:T(8,128)S(1)} %bitcast.5) | data formatting | bytes 294912 | tf_op jit(solution)/shard_map/reshape | solution.py:358
  (4 shorter events, 0.1 us)
Async XLA Ops:
  0.0 1.9 %copy-start.3 = (s32[256,12]{0,1:T(8,128)S(1)}, s32[256,12]{0,1:T(8,128)}, u32[]{:S(2)}) copy-start(s32[256,12]{0,1:T(8,128)} %param.8) | copy-start | bytes 36868
  2.5 0.9 %copy-start.2 = (f32[1,9,4096]{2,0,1:T(1,128)S(1)}, f32[1,9,4096]{2,0,1:T(1,128)}, u32[]{:S(2)}) copy-start(f32[1,9,4096]{2,0,1:T(1,128)} %param.5) | copy-start | bytes 442372
  3.4 0.8 %copy-start = (f32[3,4096]{1,0:T(4,128)S(1)}, f32[3,4096]{1,0:T(4,128)}, u32[]{:S(2)}) copy-start(f32[3,4096]{1,0:T(4,128)} %a_ref.1) | copy-start | bytes 147460
  3.4 0.9 %copy-start.1 = (f32[3,4096]{1,0:T(4,128)S(1)}, f32[3,4096]{1,0:T(4,128)}, u32[]{:S(2)}) copy-start(f32[3,4096]{1,0:T(4,128)} %start_ref.1) | copy-start | bytes 147460

commit v5 on v4

--- a/solution.py
+++ b/solution.py
@@ -199,7 +199,7 @@
             device_id_type=MESH,
         )
 
-    def interact(block, buffer):
+    def interact(block, buffer, beside):
         slots = [lists_ref[block * list_len + j] for j in range(list_len)]
         here = block_at(block)
         turned = targets[:, here].T
@@ -218,30 +218,39 @@
             lanes = slice(j * block_size, (j + 2) * block_size)
             parts[buffer, : 3 * block_size, lanes] = high
             parts[buffer, 3 * block_size :, lanes] = low
+            beside(j // 2)
 
     def weigh(block, buffer):
         slots = [lists_ref[block * list_len + j] for j in range(list_len)]
         here = block_at(block)
         weights = [table[slot, 3 * feature_rows :] for slot in slots]
-        total = lax.dot_general(
-            parts[buffer],
-            jnp.concatenate(weights, axis=1),
-            (((1,), (1,)), ((), ())),
-            preferred_element_type=jnp.float32,
-        )
-        total = total[: 3 * block_size] + total[3 * block_size :]
+        weights = jnp.concatenate(weights, axis=1)
         node_of = lax.broadcasted_iota(jnp.int32, (block_size, 3 * weight_rows), 1) // weight_rows
-        kept = jnp.zeros((block_size, 3 * weight_rows), jnp.float32)
-        for node in range(3):
-            rows = total[node * block_size : (node + 1) * block_size]
-            kept = jnp.where(node_of == node, rows, kept)
-        totals[:, here] = kept.T
+        sums = []
+
+        def part(index):
+            if index >= 6:
+                return
+            rows = slice(index * block_size, (index + 1) * block_size)
+            sums.append(
+                lax.dot_general(
+                    parts[buffer, rows],
+                    weights,
+                    (((1,), (1,)), ((), ())),
+                    preferred_element_type=jnp.float32,
+                )
+            )
+            if index == 5:
+                kept = jnp.zeros((block_size, 3 * weight_rows), jnp.float32)
+                for node in range(3):
+                    kept = jnp.where(node_of == node, sums[node] + sums[node + 3], kept)
+                totals[:, here] = kept.T
+
+        return part
 
     def two_blocks(step, carry):
-        interact(2 * step + 1, 1)
-        weigh(2 * step, 0)
-        interact(jnp.minimum(2 * step + 2, blocks - 1), 0)
-        weigh(2 * step + 1, 1)
+        interact(2 * step + 1, 1, weigh(2 * step, 0))
+        interact(jnp.minimum(2 * step + 2, blocks - 1), 0, weigh(2 * step + 1, 1))
         return carry
 
     def one_chunk(part, carry):
@@ -273,7 +282,7 @@
 
         return carry
 
-    interact(0, 0)
+    interact(0, 0, lambda part: None)
     lax.fori_loop(0, n_chunks, one_chunk, 0)
 
     def finish(part, carry):
@@ -325,7 +334,7 @@
         my_lists - me * blocks,
         blocks + (away - 1) * CAP + (my_lists != low).astype(jnp.int32),
     )
-    live_count = lax.dynamic_index_in_dim(counts, me, 0, keepdims=False)
+    live_count = jnp.sum(jnp.where(jnp.arange(groups, dtype=jnp.int32) == me, counts, 0))
     live = jnp.arange(columns, dtype=jnp.int32)[None] < live_count * block_size
 
     chunk = chunk_blocks * block_size

time: 55.6 us -> 53.5 us (0.962)
  Pallas kernels: 50.3 us -> 48.1 us
  other arithmetic: 0.64 us -> 1.95 us
  local copies, waits for them, and re-layouts: 3.72 us -> 2.47 us
    pallas_call x1, Pallas kernels: 50.3 us -> 48.1 us  [shards(): pl.pallas_call(functools.partial(kernel, n_tm, groups, radau_matrix().tol...]
    reduce_sum x0 -> x1, other arithmetic: none -> 1.3 us  [shards(): jnp.sum(jnp.where(jnp.arange(groups, dtype=jnp.int32) == me, counts, 0))]
    dynamic_slice x1 -> x0, local copies, waits for them, and re-layouts: 1.25 us -> none  [shards(): live_count = lax.dynamic_index_in_dim(counts, me, 0, keepdims=False)]
where the time goes in v5:
time: 53.5 us; the launch traced here: 53.2 us
  Pallas kernels  48.1 us (90%)
  local copies, waits for them, and re-layouts  2.47 us (5%)
  other arithmetic  1.95 us (4%)
  between operations  0.7 us (1%)
    pallas_call x1, Pallas kernels, shards(): pl.pallas_call(functools.partial(kernel, n_tm, groups, radau_matrix().tol...  48.1 us
    unnamed x10, local copies, waits for them, and re-layouts  1.39 us
    reduce_sum x1, other arithmetic, shards(): jnp.sum(jnp.where(jnp.arange(groups, dtype=jnp.int32) == me, counts, 0))  1.3 us

profile of v5, /device:TPU:0, one launch (start us, length us, event | category | flops | bytes accessed | tf_op | source)
XLA Modules:
  0.0 53.2 jit_solution(7829038848283964007)
XLA Ops:
  0.0 0.0 copy-start.3
  0.0 1.3 %fusion.12 = s32[]{:T(128)} fusion(s32[8]{0:T(128)} %param.9, s32[]{:T(128)S(6)} %axis_index.12), kind=kLoop, calls=%fused_computation.38 | loop fusion | flops 23 | bytes 40 | tf_op jit(solution)/shard_map/reduce_sum | solution.py:337
  2.0 0.0 copy-done.3
  2.0 0.1 reduce_min.26
  2.1 0.1 reduce_min.27
  2.2 0.1 reduce_max.14
  2.3 0.1 reduce_max.18
  2.4 0.1 pad_add_fusion.small_ref
  2.5 0.0 copy-start.2
  2.5 0.1 copy.9
  2.6 0.1 reshape.21
  2.8 0.1 select_reduce_fusion.3
  2.9 0.1 select_reduce_fusion.2
  3.0 0.4 copy-done.2
  3.4 0.0 copy-start
  3.4 0.0 copy-start.1
  3.4 0.1 copy.13
  3.5 0.7 %copy-done = f32[3,4096]{1,0:T(4,128)S(1)} copy-done((f32[3,4096]{1,0:T(4,128)S(1)}, f32[3,4096]{1,0:T(4,128)}, u32[]{:S(2)}) %copy-start) | copy-done | bytes 49176
  4.3 0.0 copy-done.1
  4.3 48.1 %vortex_window.1 = f32[9,4096]{1,0:T(8,128)S(1)} custom-call(s32[16]{0:T(128)S(1)} %pad_add_fusion.small_ref, s32[384]{0:T(512)S(1)} %fusion.9.lists_ref, f32[9,4096]{1,0:T(8,128)S(1)} %bitcast.5, f32[3,4096]{1,0:T(4,128)S(1)} %copy-done, f32[3,4096]{1,0:T(4,128)S(1)} %copy-done.1, f32[1,4096]{1,0:T(1,128)S(1)} %compare_convert_fusion.live_ref), custom_call_target="tpu_custom_call" | custom-call | tf_op jit(solution)/shard_map/vortex_window/pallas_call | solution.py:341
  52.4 0.8 %copy.10 = f32[1,9,4096]{2,0,1:T(1,128)} copy(f32[1,9,4096]{2,1,0:T(8,128)S(1)} %bitcast.4) | data formatting | bytes 294912 | tf_op jit(solution)/shard_map/reshape | solution.py:367
  (4 shorter events, 0.1 us)
Async XLA Ops:
  0.0 2.0 %copy-start.3 = (s32[256,12]{0,1:T(8,128)S(1)}, s32[256,12]{0,1:T(8,128)}, u32[]{:S(2)}) copy-start(s32[256,12]{0,1:T(8,128)} %param.8) | copy-start | bytes 36868
  2.5 0.9 %copy-start.2 = (f32[1,9,4096]{2,0,1:T(1,128)S(1)}, f32[1,9,4096]{2,0,1:T(1,128)}, u32[]{:S(2)}) copy-start(f32[1,9,4096]{2,0,1:T(1,128)} %param.5) | copy-start | bytes 442372
  3.4 0.8 %copy-start = (f32[3,4096]{1,0:T(4,128)S(1)}, f32[3,4096]{1,0:T(4,128)}, u32[]{:S(2)}) copy-start(f32[3,4096]{1,0:T(4,128)} %a_ref.1) | copy-start | bytes 147460
  3.4 0.9 %copy-start.1 = (f32[3,4096]{1,0:T(4,128)S(1)}, f32[3,4096]{1,0:T(4,128)}, u32[]{:S(2)}) copy-start(f32[3,4096]{1,0:T(4,128)} %start_ref.1) | copy-start | bytes 147460

commit v6 on v5

--- a/solution.py
+++ b/solution.py
@@ -16,6 +16,7 @@
 feature_rows = 32
 weight_rows = 16
 chunk_blocks = 8
+direct_pairs = (1, 3, 5)
 MESH = pl.DeviceIdType.MESH
 
 
@@ -102,6 +103,7 @@
     stage,
     landed,
     table,
+    places,
     targets,
     parts,
     totals,
@@ -164,7 +166,9 @@
         rows = [as_source for _, as_source in pairs] + weights
         rows = jnp.concatenate(rows, axis=0).astype(jnp.bfloat16)
         for k in range(count):
-            table[slot + k] = rows[:, k * block_size : (k + 1) * block_size]
+            lanes = slice(k * block_size, (k + 1) * block_size)
+            table[slot + k] = rows[:, lanes]
+            places[slot + k] = pos[:, lanes]
         return jnp.concatenate([as_target for as_target, _ in pairs], axis=0)
 
     own_step = 4
@@ -199,6 +203,16 @@
             device_id_type=MESH,
         )
 
+    def direct(spots, sources):
+        rows = []
+        for node in range(3):
+            distance = core_sq
+            for c in range(3 * node, 3 * node + 3):
+                offset = spots[c] - sources[c : c + 1]
+                distance = offset * offset + distance
+            rows.append(distance)
+        return jnp.concatenate(rows, axis=0)
+
     def interact(block, buffer, beside):
         slots = [lists_ref[block * list_len + j] for j in range(list_len)]
         here = block_at(block)
@@ -206,11 +220,20 @@
         node_of = lax.broadcasted_iota(jnp.int32, turned.shape, 1) // feature_rows
         lhs = [jnp.where(node_of == node, turned, 0.0) for node in range(3)]
         lhs = jnp.concatenate(lhs, axis=0).astype(jnp.bfloat16)
+        own_places = places[block].T
+        spots = [
+            jnp.broadcast_to(own_places[:, row : row + 1], (block_size, block_size))
+            for row in range(9)
+        ]
         for j in range(0, list_len, 2):
-            pair = [table[slot, : 3 * feature_rows] for slot in slots[j : j + 2]]
-            distance = jnp.dot(
-                lhs, jnp.concatenate(pair, axis=1), preferred_element_type=jnp.float32
-            )
+            if j // 2 in direct_pairs:
+                distance = [direct(spots, places[slot]) for slot in slots[j : j + 2]]
+                distance = jnp.concatenate(distance, axis=1)
+            else:
+                pair = [table[slot, : 3 * feature_rows] for slot in slots[j : j + 2]]
+                distance = jnp.dot(
+                    lhs, jnp.concatenate(pair, axis=1), preferred_element_type=jnp.float32
+                )
             inverse = lax.rsqrt(distance)
             value = inverse * inverse * inverse
             high = value.astype(jnp.bfloat16)
@@ -349,6 +372,7 @@
             pltpu.VMEM((groups, 12, CAP * block_size), jnp.float32),
             pltpu.VMEM((groups, 12, CAP * block_size), jnp.float32),
             pltpu.VMEM((slots, 3 * (feature_rows + weight_rows), block_size), jnp.bfloat16),
+            pltpu.VMEM((slots, 9, block_size), jnp.float32),
             pltpu.VMEM((3 * feature_rows, columns), jnp.float32),
             pltpu.VMEM((2, 6 * block_size, lists.shape[1] * block_size), jnp.bfloat16),
             pltpu.VMEM((3 * weight_rows, columns), jnp.float32),

time: 53.5 us -> 60.1 us (1.12)
  Pallas kernels: 48.1 us -> 54.7 us
    pallas_call x1, Pallas kernels: 48.1 us -> 54.7 us  [shards(): pl.pallas_call(functools.partial(kernel, n_tm, groups, radau_matrix().tol...]
where the time goes in v6:
time: 60.1 us; the launch traced here: 59.8 us
  Pallas kernels  54.7 us (91%)
  local copies, waits for them, and re-layouts  2.47 us (4%)
  other arithmetic  1.95 us (3%)
  between operations  0.7 us (1%)
    pallas_call x1, Pallas kernels, shards(): pl.pallas_call(functools.partial(kernel, n_tm, groups, radau_matrix().tol...  54.7 us
    unnamed x10, local copies, waits for them, and re-layouts  1.39 us
    reduce_sum x1, other arithmetic, shards(): jnp.sum(jnp.where(jnp.arange(groups, dtype=jnp.int32) == me, counts, 0))  1.3 us

profile of v6, /device:TPU:0, one launch (start us, length us, event | category | flops | bytes accessed | tf_op | source)
XLA Modules:
  0.0 59.8 jit_solution(1256908595927042470)
XLA Ops:
  0.0 0.0 copy-start.3
  0.0 1.3 %fusion.12 = s32[]{:T(128)} fusion(s32[8]{0:T(128)} %param.9, s32[]{:T(128)S(6)} %axis_index.12), kind=kLoop, calls=%fused_computation.38 | loop fusion | flops 23 | bytes 40 | tf_op jit(solution)/shard_map/reduce_sum | solution.py:360
  2.0 0.0 copy-done.3
  2.0 0.1 reduce_min.26
  2.1 0.1 reduce_min.27
  2.2 0.1 reduce_max.14
  2.3 0.1 reduce_max.18
  2.4 0.1 pad_add_fusion.small_ref
  2.5 0.0 copy-start.2
  2.5 0.1 copy.9
  2.6 0.1 reshape.21
  2.8 0.1 select_reduce_fusion.3
  2.9 0.1 select_reduce_fusion.2
  3.0 0.4 copy-done.2
  3.4 0.0 copy-start
  3.4 0.0 copy-start.1
  3.4 0.1 copy.13
  3.5 0.7 %copy-done = f32[3,4096]{1,0:T(4,128)S(1)} copy-done((f32[3,4096]{1,0:T(4,128)S(1)}, f32[3,4096]{1,0:T(4,128)}, u32[]{:S(2)}) %copy-start) | copy-done | bytes 49176
  4.3 0.0 copy-done.1
  4.3 54.7 %vortex_window.1 = f32[9,4096]{1,0:T(8,128)S(1)} custom-call(s32[16]{0:T(128)S(1)} %pad_add_fusion.small_ref, s32[384]{0:T(512)S(1)} %fusion.9.lists_ref, f32[9,4096]{1,0:T(8,128)S(1)} %bitcast.5, f32[3,4096]{1,0:T(4,128)S(1)} %copy-done, f32[3,4096]{1,0:T(4,128)S(1)} %copy-done.1, f32[1,4096]{1,0:T(1,128)S(1)} %compare_convert_fusion.live_ref), custom_call_target="tpu_custom_call" | custom-call | tf_op jit(solution)/shard_map/vortex_window/pallas_call | solution.py:364
  59.0 0.8 %copy.10 = f32[1,9,4096]{2,0,1:T(1,128)} copy(f32[1,9,4096]{2,1,0:T(8,128)S(1)} %bitcast.4) | data formatting | bytes 294912 | tf_op jit(solution)/shard_map/reshape | solution.py:391
  (4 shorter events, 0.1 us)
Async XLA Ops:
  0.0 2.0 %copy-start.3 = (s32[256,12]{0,1:T(8,128)S(1)}, s32[256,12]{0,1:T(8,128)}, u32[]{:S(2)}) copy-start(s32[256,12]{0,1:T(8,128)} %param.8) | copy-start | bytes 36868
  2.5 0.9 %copy-start.2 = (f32[1,9,4096]{2,0,1:T(1,128)S(1)}, f32[1,9,4096]{2,0,1:T(1,128)}, u32[]{:S(2)}) copy-start(f32[1,9,4096]{2,0,1:T(1,128)} %param.5) | copy-start | bytes 442372
  3.4 0.8 %copy-start = (f32[3,4096]{1,0:T(4,128)S(1)}, f32[3,4096]{1,0:T(4,128)}, u32[]{:S(2)}) copy-start(f32[3,4096]{1,0:T(4,128)} %a_ref.1) | copy-start | bytes 147460
  3.4 0.9 %copy-start.1 = (f32[3,4096]{1,0:T(4,128)S(1)}, f32[3,4096]{1,0:T(4,128)}, u32[]{:S(2)}) copy-start(f32[3,4096]{1,0:T(4,128)} %start_ref.1) | copy-start | bytes 147460
